TPU v7x, 32 devices: a whole 2x2x4 slice. The times are simulated.
32 devices in a mesh: gx: 4 (over y, core), gy: 2 (over x), gz: 4 (over z).
Axes of the slice: x: 2, y: 2, z: 4, core: 2. Of those that a mesh axis runs over, the one named last changes fastest.
Arguments:
- stem: bfloat16 [2, 4, 2, 4, 256, 1024], P(None, 'gx', 'gy', 'gz'), may hold values from -6 to 6
- branch_one: bfloat16 [2, 2, 1024, 1024], replicated, may hold values from -0.125 to 0.125
- branch_two: bfloat16 [2, 2, 1024, 1024], P(None, None, ('gy', 'gz')), may hold values from -0.1875 to 0.1875
- branch_three: bfloat16 [2, 2, 1024, 1024], P(None, None, 'gz'), may hold values from -0.125 to 0.125
- slice_values: int32 [3], replicated, may hold values from 0 to 1, as said below
Outputs:
- contracted: bfloat16 [2, 4, 2, 4, 256, 1024], P(None, 'gx', 'gy', 'gz')
Inputs may be any that keep to these rules, and one draw needn't show every extreme that they name: `slice_values`: the first two slices differ.
All inputs are finite; a program needn't handle non-finite values.
Results may differ from a plain program's by a relative error of at most 0.0057.
Values may be sent and summed in bfloat16 or wider, within the bound.
A program may use at most 128 MiB of HBM per device.

v0:
```python
import functools

import jax
import jax.numpy as jnp
from jax import lax
from jax.experimental import pallas as pl
from jax.experimental.pallas import tpu as pltpu
from jax.sharding import PartitionSpec as P

WIDTH = 1024
ROWS = 256


def complex_matrix(branch):
    top_half = jnp.concatenate([branch[0], branch[1]], axis=1)
    bottom_half = jnp.concatenate([-branch[1], branch[0]], axis=1)
    return jnp.concatenate([top_half, bottom_half], axis=0)


def complex_product(operand, branch):
    joined = jnp.concatenate([operand[0], operand[1]], axis=1)
    result = jnp.dot(joined, complex_matrix(branch), preferred_element_type=jnp.float32)
    columns = branch.shape[2]
    return jnp.stack([result[:, :columns], result[:, columns:]])


def split_result(result):
    columns = result.shape[1] // 2
    return jnp.stack([result[:, :columns], result[:, columns:]])


def make_accumulate(operand, shard_rows):
    real_part = operand[0]
    imag_part = operand[1]
    joined = jnp.concatenate([real_part, imag_part], axis=1)
    return jnp.dot(joined, complex_matrix(shard_rows), preferred_element_type=jnp.float32)


def third_contraction(operand, branch_three, slice_values):
    local_third = lax.dynamic_index_in_dim(branch_three, slice_values[2], 0, keepdims=False)
    summed = make_accumulate(operand, lax.all_gather(local_third, "gz", axis=1, tiled=True))
    return split_result(summed).astype(jnp.bfloat16)


def body(stem, branch_one, branch_two, branch_three, slice_values):
    count_gx = lax.axis_size("gx")
    count_gy = lax.axis_size("gy")
    count_gz = lax.axis_size("gz")
    group_one = count_gx * count_gy
    group_two = count_gy * count_gz
    rows_one = ROWS // group_one
    rows_two = ROWS // group_two
    part_one = WIDTH // group_one
    part_two = WIDTH // group_two
    first_branch = lax.dynamic_index_in_dim(branch_one, slice_values[0], 0, keepdims=False)
    arrived = lax.all_to_all(
        stem.reshape(2, 1, group_one, rows_one, WIDTH),
        ("gx", "gy"),
        split_axis=2,
        concat_axis=1,
        tiled=True,
    )
    ordered = arrived.reshape(2, group_one, rows_one, part_one, group_one).transpose(0, 2, 4, 1, 3)
    ordered = ordered.reshape(2, ROWS, WIDTH)
    middle = complex_product(ordered, first_branch).astype(jnp.bfloat16)
    gathered = lax.all_to_all(
        middle.reshape(2, group_two, 1, rows_two, WIDTH),
        ("gy", "gz"),
        split_axis=1,
        concat_axis=2,
        tiled=True,
    )
    regrouped = gathered.reshape(2, group_two, rows_two, part_two, group_two).transpose(
        0, 2, 4, 1, 3
    )
    regrouped = regrouped.reshape(2, ROWS, WIDTH)
    local_second = lax.dynamic_index_in_dim(branch_two, slice_values[1], 0, keepdims=False)
    summed = make_accumulate(
        regrouped, lax.all_gather(local_second, ("gy", "gz"), axis=1, tiled=True)
    )
    second = split_result(summed).astype(jnp.bfloat16)
    returned = lax.all_to_all(
        second.reshape(2, 1, rows_two, group_two, group_two, part_two),
        ("gy", "gz"),
        split_axis=4,
        concat_axis=1,
        tiled=True,
    )
    result = third_contraction(returned.reshape(2, ROWS, WIDTH), branch_three, slice_values)
    return result.reshape(stem.shape)


MESH = pl.DeviceIdType.MESH
VMEM_LIMIT = 56 * 1024 * 1024
TILE = 256
LANE = 128


def complex_tile(lhs, rhs):
    result = jnp.dot(lhs, rhs, preferred_element_type=jnp.float32)
    m, n = result.shape[0] // 2, result.shape[1] // 2
    real = result[:m, :n] - result[m:, n:]
    imag = result[m:, :n] + result[:m, n:]
    return real.astype(jnp.bfloat16), imag.astype(jnp.bfloat16)


def kernel(
    dims, slices, stem, one_hbm, two_in, three_in, out,
    perm, one, one_perm, two, three, sorted_stem, first, second, third, result,
    one_sem, own_sem, stem_send, stem_recv, part_send, part_recv, z_send, z_recv, back_send, back_recv,
):
    nx, ny, nz = dims
    group = ny * nz
    devices = nx * group
    gx, gy, gz = lax.axis_index("gx"), lax.axis_index("gy"), lax.axis_index("gz")
    line, core = gx // 2, gx % 2
    me = (gx * ny + gy) * nz + gz
    place = gy * nz + gz

    load_one = pltpu.make_async_copy(one_hbm, one, one_sem)
    load_one.start()

    def coordinates(index):
        return (index // group, (index // nz) % ny, index % nz)

    barrier = pltpu.get_barrier_semaphore()

    def greet(step, carry):
        pl.semaphore_signal(
            barrier, inc=1, device_id=coordinates((me + step) % devices), device_id_type=MESH
        )
        return carry

    lax.fori_loop(1, devices, greet, 0)

    rows_two, rows_three = WIDTH // group, WIDTH // nz
    piece = rows_two // nx
    two[:, pl.ds(pl.multiple_of(place * rows_two, rows_two), rows_two), :] = two_in[slices[1]]
    three[:, pl.ds(pl.multiple_of(gz * rows_three, rows_three), rows_three), :] = three_in[slices[2]]

    def make_perm(tile, carry):
        column = lax.broadcasted_iota(jnp.int32, (WIDTH, TILE), 1) + tile * TILE
        row = lax.broadcasted_iota(jnp.int32, (WIDTH, TILE), 0)
        wanted = (column % LANE) * group + column // LANE
        perm[tile] = jnp.where(row == wanted, 1.0, 0.0).astype(jnp.bfloat16)
        return carry

    lax.fori_loop(0, WIDTH // TILE, make_perm, 0)
    pl.semaphore_wait(barrier, devices - 1)

    sends = []

    upper = gz // 2
    depth = gz + upper * (nz - 1 - 2 * gz)

    def mirrored(position):
        return position + upper * (nz - 1 - 2 * position)

    def z_of(back):
        return gz if back == 0 else mirrored(1 - depth if back == 1 else back)

    def piece_two_of(line_of, x, back):
        start = (x * nz + z_of(back)) * rows_two + (line_of * 2 + core) * piece
        return two.at[:, pl.ds(pl.multiple_of(start, piece), piece), :]

    def piece_three_of(line_of, x, back):
        start = z_of(back) * rows_three + ((line_of * 2 + core) * ny + x) * piece
        return three.at[:, pl.ds(pl.multiple_of(start, piece), piece), :]

    def send(ref, device):
        index = len(sends)
        copy = pltpu.make_async_remote_copy(
            src_ref=ref, dst_ref=ref,
            send_sem=part_send.at[index], recv_sem=part_recv.at[index],
            device_id=device, device_id_type=MESH,
        )
        copy.start()
        sends.append(copy)
        return copy

    other_line, other_x = 1 - line, 1 - gy
    to_line = (other_line * 2 + core, gy, gz)
    to_x = (gx, other_x, gz)
    to_core = (line * 2 + 1 - core, gy, gz)

    pieces_of = (piece_two_of, piece_three_of)

    def z_copy(kind, back, hop, position):
        ref = pieces_of[kind](line, gy, back)
        return pltpu.make_async_remote_copy(
            src_ref=ref, dst_ref=ref,
            send_sem=z_send.at[kind, hop], recv_sem=z_recv.at[kind, z_of(back)],
            device_id=(gx, gy, mirrored(position)), device_id_type=MESH,
        )

    def z_hops(back):
        return [z_copy(kind, back, 1 + back, 2 if back < 2 else 0) for kind in range(2)]

    for kind in range(2):
        z_copy(kind, 0, 0, 1 - depth).start()

    @pl.when(depth == 1)
    def _():
        for copy in z_hops(0):
            copy.start()

    def pass_on(back):
        for kind in range(2):
            z_copy(kind, back, 0, 0).wait_recv()

        @pl.when(depth == 1)
        def _():
            for copy in z_hops(back):
                copy.start()

    two_y, three_y, three_x = {}, {}, {}
    two_core, three_core = [], []
    two_x = {0: send(piece_two_of(line, gy, 0), to_x)}

    def sort_stem(tile, carry):
        operand = stem[...].reshape(2 * ROWS, WIDTH)
        moved = jnp.dot(operand, perm[tile], preferred_element_type=jnp.float32)
        moved = moved.astype(jnp.bfloat16).reshape(2, ROWS, TILE)
        sorted_stem[:, :, pl.ds(pl.multiple_of(tile * TILE, TILE), TILE)] = moved
        return carry

    lax.fori_loop(0, WIDTH // TILE, sort_stem, 0)
    rows_one = ROWS // nx

    def stem_block(index):
        return sorted_stem.at[
            :,
            pl.ds(pl.multiple_of((index // group) * rows_one, rows_one), rows_one),
            pl.ds(pl.multiple_of((index % group) * LANE, LANE), LANE),
        ]

    def landing(index):
        return first.at[:, index % nz, :, pl.ds(pl.multiple_of((index // nz) * LANE, LANE), LANE)]

    def stem_copy(step):
        target = (me + step) % devices
        return pltpu.make_async_remote_copy(
            src_ref=stem_block(target), dst_ref=landing(me),
            send_sem=stem_send.at[step], recv_sem=stem_recv.at[step],
            device_id=coordinates(target), device_id_type=MESH,
        )

    def send_plane(step, carry):
        stem_copy(step * nz).start()
        return carry

    def send_stem_rest(step, carry):
        stem_copy(step + step // (nz - 1) + 1).start()
        return carry

    lax.fori_loop(1, devices // nz, send_plane, 0)
    own = pltpu.make_async_copy(stem_block(me), landing(me), own_sem.at[0])
    own.start()

    for step in range(1, nz):
        pass_on(step)
        two_x[step] = send(piece_two_of(line, gy, step), to_x)
        three_y[step] = send(piece_three_of(line, gy, step), to_line)
    for step in range(1, nz):
        two_y[0, step] = send(piece_two_of(line, gy, step), to_line)
        three_x[0, step] = send(piece_three_of(line, gy, step), to_x)
    lax.fori_loop(0, devices - devices // nz, send_stem_rest, 0)
    for step in range(1, nz):
        two_core.append(send(piece_two_of(line, gy, step), to_core))
        three_core.append(send(piece_three_of(line, gy, step), to_core))

    load_one.wait()

    def sort_one(tile, carry):
        for part in range(2):
            moved = jnp.dot(
                one[slices[0], part], perm[tile], preferred_element_type=jnp.float32
            ).astype(jnp.bfloat16)
            for half in range(2):
                one_perm[2 * tile + half, :, part * LANE : (part + 1) * LANE] = moved[
                    :, half * LANE : (half + 1) * LANE
                ]
        return carry

    lax.fori_loop(0, WIDTH // TILE, sort_one, 0)

    for step in range(nz):
        two_x[step].wait_recv()
        two_y[1, step] = send(piece_two_of(line, other_x, step), to_line)
        two_core.append(send(piece_two_of(line, other_x, step), to_core))
        if step > 0:
            three_y[step].wait_recv()
            three_x[1, step] = send(piece_three_of(other_line, gy, step), to_x)
            three_core.append(send(piece_three_of(other_line, gy, step), to_core))

    own.wait()

    def await_stem(step, carry):
        stem_copy(step).wait_recv()
        return carry

    lax.fori_loop(1, devices, await_stem, 0)
    chunk = ROWS // group

    def contract_first(k, carry):
        operand = first[...].reshape(2 * ROWS, WIDTH)
        for part, value in enumerate(complex_tile(operand, one_perm[k])):
            for c in range(nz):
                for ry in range(ny):
                    row, column = (c * ny + ry) * chunk, (ry * nz + c) * LANE
                    second[part, k, :, column : column + LANE] = value[row : row + chunk]
        return carry

    lax.fori_loop(0, group, contract_first, 0)

    for step in range(1, nz):
        two_y[0, step].wait_recv()
        two_core.append(send(piece_two_of(other_line, gy, step), to_core))
        three_x[0, step].wait_recv()
        three_core.append(send(piece_three_of(line, other_x, step), to_core))
    for step in range(nz):
        two_y[1, step].wait_recv()
        two_core.append(send(piece_two_of(other_line, other_x, step), to_core))
        if step > 0:
            three_x[1, step].wait_recv()
            three_core.append(send(piece_three_of(other_line, other_x, step), to_core))

    for copy in two_core:
        copy.wait_recv()

    def contract_second(s, carry):
        operand = second[...].reshape(2 * ROWS, WIDTH)
        columns = pl.ds(pl.multiple_of(s * LANE, LANE), LANE)
        branch = jnp.concatenate([two[0, :, columns], two[1, :, columns]], axis=1)
        for part, value in enumerate(complex_tile(operand, branch)):
            for k in range(group):
                third[part, s, :, k * LANE : (k + 1) * LANE] = value[k * chunk : (k + 1) * chunk]
        return carry

    lax.fori_loop(0, group, contract_second, 0)

    for copy in three_core:
        copy.wait_recv()
    tiles = WIDTH // TILE

    def back_copy(tile, step):
        target = (place + step) % group
        columns = pl.ds(pl.multiple_of(tile * TILE, TILE), TILE)
        return pltpu.make_async_remote_copy(
            src_ref=result.at[target, :, :, columns], dst_ref=out.at[place, :, :, columns],
            send_sem=back_send.at[tile, step], recv_sem=back_recv.at[tile, step],
            device_id=(gx, target // nz, target % nz), device_id_type=MESH,
        )

    def contract_third(tile, carry):
        operand = third[...].reshape(2 * ROWS, WIDTH)
        columns = pl.ds(pl.multiple_of(tile * TILE, TILE), TILE)
        branch = jnp.concatenate([three[0, :, columns], three[1, :, columns]], axis=1)
        for part, value in enumerate(complex_tile(operand, branch)):
            result[:, part, :, columns] = value.reshape(group, chunk, TILE)

        def send_back(step, inner):
            back_copy(tile, step).start()
            return inner

        lax.fori_loop(1, group, send_back, 0)
        return carry

    lax.fori_loop(0, tiles, contract_third, 0)
    keep = pltpu.make_async_copy(result.at[place], out.at[place], own_sem.at[1])
    keep.start()
    keep.wait()

    for copy in sends:
        copy.wait_send()
    for kind in range(2):
        z_copy(kind, 0, 0, 1 - depth).wait_send()

    @pl.when(depth == 1)
    def _():
        for back in range(nz):
            for copy in z_hops(back):
                copy.wait_send()

    def end_stem(step, carry):
        stem_copy(step).wait_send()
        return carry

    lax.fori_loop(1, devices, end_stem, 0)

    def end_back(index, carry):
        copy = back_copy(index // (group - 1), index % (group - 1) + 1)
        copy.wait_send()
        copy.wait_recv()
        return carry

    lax.fori_loop(0, tiles * (group - 1), end_back, 0)


def fused_body(dims, stem, branch_one, branch_two, branch_three, slice_values):
    nx, ny, nz = dims
    group = ny * nz
    devices = nx * group
    chunk = ROWS // group
    pieces = nz + (nz - 1) + (2 * nz - 1) + 2 * (nz - 1)
    pieces = pieces + 2 * (2 * nz - 1) + 4 * (nz - 1)
    bf16 = jnp.bfloat16
    vmem = pl.BlockSpec(memory_space=pltpu.VMEM)
    dma = pltpu.SemaphoreType.DMA
    blocks = pl.pallas_call(
        functools.partial(kernel, dims),
        out_shape=jax.ShapeDtypeStruct((group, 2, chunk, WIDTH), bf16),
        in_specs=[
            pl.BlockSpec(memory_space=pltpu.SMEM),
            vmem,
            pl.BlockSpec(memory_space=pl.ANY),
            vmem,
            vmem,
        ],
        out_specs=pl.BlockSpec(memory_space=pl.ANY),
        scratch_shapes=[
            pltpu.VMEM((WIDTH // TILE, WIDTH, TILE), bf16),
            pltpu.VMEM(branch_one.shape, bf16),
            pltpu.VMEM((group, WIDTH, 2 * LANE), bf16),
            pltpu.VMEM((2, WIDTH, WIDTH), bf16),
            pltpu.VMEM((2, WIDTH, WIDTH), bf16),
            pltpu.VMEM((2, ROWS, WIDTH), bf16),
            pltpu.VMEM((2, nz, ROWS // nx, WIDTH), bf16),
            pltpu.VMEM((2, group, chunk, WIDTH), bf16),
            pltpu.VMEM((2, group, chunk, WIDTH), bf16),
            pltpu.VMEM((group, 2, chunk, WIDTH), bf16),
            dma,
            dma((2,)),
            dma((devices,)),
            dma((devices,)),
            dma((pieces,)),
            dma((pieces,)),
            dma((2, nz + 1)),
            dma((2, nz)),
            dma((WIDTH // TILE, group)),
            dma((WIDTH // TILE, group)),
        ],
        compiler_params=pltpu.CompilerParams(
            collective_id=0, has_side_effects=True, vmem_limit_bytes=VMEM_LIMIT
        ),
        cost_estimate=pl.CostEstimate(
            flops=24 * ROWS * WIDTH * WIDTH, bytes_accessed=16 * WIDTH * WIDTH, transcendentals=0
        ),
    )(slice_values, stem.reshape(2, ROWS, WIDTH), branch_one, branch_two, branch_three)
    return blocks.transpose(1, 2, 0, 3).reshape(stem.shape)


def solution(mesh):
    dims = (mesh.shape["gx"], mesh.shape["gy"], mesh.shape["gz"])
    group_one, group_two = dims[0] * dims[1], dims[1] * dims[2]
    fused = group_one == group_two == WIDTH // LANE and dims == (4, 2, 4)
    return jax.shard_map(
        functools.partial(fused_body, dims) if fused else body,
        mesh=mesh,
        in_specs=(
            P(None, "gx", "gy", "gz", None, None),
            P(),
            P(None, None, ("gy", "gz"), None),
            P(None, None, "gz", None),
            P(),
        ),
        out_specs=P(None, "gx", "gy", "gz", None, None),
        check_vma=False,
    )
```

profile of v0, /device:TPU:0, one launch (start us, length us, event | category | flops | bytes accessed | tf_op | source)
XLA Modules:
  0.0 90.5 jit_solution(16377448410785130564)
XLA Ops:
  0.0 87.7 %shard_map.55 = bf16[8,2,32,1024]{3,2,1,0:T(8,128)(2,1)} custom-call(s32[3]{0:T(128)} %slices.1, bf16[2,256,1024]{2,1,0:T(8,128)(2,1)} %bitcast.8, bf16[2,2,1024,1024]{3,2,1,0:T(8,128)(2,1)} %one_hbm.1, bf16[2,2,128,1024]{3,2,1,0:T(8,128)(2,1)} %two_in.1, bf16[2,2,256,1024]{3,2,1,0:T(8,128)(2,1)} %three_in.1), custom_call_target="tpu_custom_call" | custom-call | flops 6442450944 | bytes 16777216 | tf_op jit(solution)/shard_map/pallas_call | solution.py:410
  87.7 2.8 %copy.9 = bf16[2,32,8,1024]{3,2,1,0:T(8,128)(2,1)} copy(bf16[2,32,8,1024]{3,1,0,2:T(8,128)(2,1)} %bitcast.7) | data formatting | bytes 2097152 | tf_op jit(solution)/shard_map/transpose | solution.py:450
where the time goes:
time: 91.9 us; the launch traced here: 90.5 us
  Pallas kernels  87.7 us (95%)
  local copies, waits for them, and re-layouts  2.77 us (3%)
    pallas_call x1, Pallas kernels, fused_body(): pl.pallas_call(functools.partial(kernel, dims), out_shape=jax.ShapeDtypeS...  87.7 us
    transpose x1, local copies, waits for them, and re-layouts, fused_body(): return blocks.transpose(1, 2, 0, 3).reshape(stem.shape)  2.77 us

commit v1 on v0

v1 whole, which is shorter than its diff:
```python
import functools

import jax
import jax.numpy as jnp
from jax import lax
from jax.experimental import pallas as pl
from jax.experimental.pallas import tpu as pltpu
from jax.sharding import PartitionSpec as P

WIDTH = 1024
ROWS = 256


def complex_matrix(branch):
    top_half = jnp.concatenate([branch[0], branch[1]], axis=1)
    bottom_half = jnp.concatenate([-branch[1], branch[0]], axis=1)
    return jnp.concatenate([top_half, bottom_half], axis=0)


def complex_product(operand, branch):
    joined = jnp.concatenate([operand[0], operand[1]], axis=1)
    result = jnp.dot(joined, complex_matrix(branch), preferred_element_type=jnp.float32)
    columns = branch.shape[2]
    return jnp.stack([result[:, :columns], result[:, columns:]])


def split_result(result):
    columns = result.shape[1] // 2
    return jnp.stack([result[:, :columns], result[:, columns:]])


def make_accumulate(operand, shard_rows):
    real_part = operand[0]
    imag_part = operand[1]
    joined = jnp.concatenate([real_part, imag_part], axis=1)
    return jnp.dot(joined, complex_matrix(shard_rows), preferred_element_type=jnp.float32)


def third_contraction(operand, branch_three, slice_values):
    local_third = lax.dynamic_index_in_dim(branch_three, slice_values[2], 0, keepdims=False)
    summed = make_accumulate(operand, lax.all_gather(local_third, "gz", axis=1, tiled=True))
    return split_result(summed).astype(jnp.bfloat16)


def body(stem, branch_one, branch_two, branch_three, slice_values):
    count_gx = lax.axis_size("gx")
    count_gy = lax.axis_size("gy")
    count_gz = lax.axis_size("gz")
    group_one = count_gx * count_gy
    group_two = count_gy * count_gz
    rows_one = ROWS // group_one
    rows_two = ROWS // group_two
    part_one = WIDTH // group_one
    part_two = WIDTH // group_two
    first_branch = lax.dynamic_index_in_dim(branch_one, slice_values[0], 0, keepdims=False)
    arrived = lax.all_to_all(
        stem.reshape(2, 1, group_one, rows_one, WIDTH),
        ("gx", "gy"),
        split_axis=2,
        concat_axis=1,
        tiled=True,
    )
    ordered = arrived.reshape(2, group_one, rows_one, part_one, group_one).transpose(0, 2, 4, 1, 3)
    ordered = ordered.reshape(2, ROWS, WIDTH)
    middle = complex_product(ordered, first_branch).astype(jnp.bfloat16)
    gathered = lax.all_to_all(
        middle.reshape(2, group_two, 1, rows_two, WIDTH),
        ("gy", "gz"),
        split_axis=1,
        concat_axis=2,
        tiled=True,
    )
    regrouped = gathered.reshape(2, group_two, rows_two, part_two, group_two).transpose(
        0, 2, 4, 1, 3
    )
    regrouped = regrouped.reshape(2, ROWS, WIDTH)
    local_second = lax.dynamic_index_in_dim(branch_two, slice_values[1], 0, keepdims=False)
    summed = make_accumulate(
        regrouped, lax.all_gather(local_second, ("gy", "gz"), axis=1, tiled=True)
    )
    second = split_result(summed).astype(jnp.bfloat16)
    returned = lax.all_to_all(
        second.reshape(2, 1, rows_two, group_two, group_two, part_two),
        ("gy", "gz"),
        split_axis=4,
        concat_axis=1,
        tiled=True,
    )
    result = third_contraction(returned.reshape(2, ROWS, WIDTH), branch_three, slice_values)
    return result.reshape(stem.shape)


MESH = pl.DeviceIdType.MESH
VMEM_LIMIT = 56 * 1024 * 1024
TILE = 256
LANE = 128


def complex_tile(lhs, rhs):
    result = jnp.dot(lhs, rhs, preferred_element_type=jnp.float32)
    m, n = result.shape[0] // 2, result.shape[1] // 2
    real = result[:m, :n] - result[m:, n:]
    imag = result[m:, :n] + result[:m, n:]
    return real.astype(jnp.bfloat16), imag.astype(jnp.bfloat16)


TILES = WIDTH // TILE


def kernel(
    dims, slices, stem, one_hbm, two_in, three_in, out,
    perm, one, one_perm, two, three, sorted_stem, first, second, third, result,
    local_sem, z_recv, two_recv, three_recv, bulk_recv, sent,
):
    nx, ny, nz = dims
    group = ny * nz
    devices = nx * group
    gx, gy, gz = lax.axis_index("gx"), lax.axis_index("gy"), lax.axis_index("gz")
    line, core = gx // 2, gx % 2
    me = (gx * ny + gy) * nz + gz
    place = gy * nz + gz

    load_one = pltpu.make_async_copy(one_hbm, one, local_sem.at[0])
    load_one.start()

    def coordinates(index):
        return (index // group, (index // nz) % ny, index % nz)

    barrier = pltpu.get_barrier_semaphore()

    def greet(step, carry):
        pl.semaphore_signal(
            barrier, inc=1, device_id=coordinates((me + step) % devices), device_id_type=MESH
        )
        return carry

    lax.fori_loop(1, devices, greet, 0)

    rows_two, rows_three = WIDTH // group, WIDTH // nz
    piece = rows_two // nx
    two[:, pl.ds(pl.multiple_of(place * rows_two, rows_two), rows_two), :] = two_in[slices[1]]
    own_rows = pl.ds(pl.multiple_of(gz * rows_three, rows_three), rows_three)
    for tile in range(TILES):
        three[tile, :, own_rows, :] = three_in[slices[2], :, :, tile * TILE : (tile + 1) * TILE]

    def make_perm(tile, carry):
        column = lax.broadcasted_iota(jnp.int32, (WIDTH, TILE), 1) + tile * TILE
        row = lax.broadcasted_iota(jnp.int32, (WIDTH, TILE), 0)
        wanted = (column % LANE) * group + column // LANE
        perm[tile] = jnp.where(row == wanted, 1.0, 0.0).astype(jnp.bfloat16)
        return carry

    lax.fori_loop(0, TILES, make_perm, 0)
    rows_one = ROWS // nx

    def sort_stem(tile, carry):
        operand = stem[...].reshape(2 * ROWS, WIDTH)
        moved = jnp.dot(operand, perm[tile], preferred_element_type=jnp.float32)
        moved = moved.astype(jnp.bfloat16).reshape(2, nx, rows_one, TILE)
        for x in range(nx):
            for half in range(2):
                sorted_stem[x * group + 2 * tile + half] = moved[
                    :, x, :, half * LANE : (half + 1) * LANE
                ]
        return carry

    lax.fori_loop(0, TILES, sort_stem, 0)
    pl.semaphore_wait(barrier, devices - 1)

    upper = gz // 2
    depth = gz + upper * (nz - 1 - 2 * gz)

    def mirrored(position):
        return position + upper * (nz - 1 - 2 * position)

    def z_of(back):
        return gz if back == 0 else mirrored(1 - depth if back == 1 else back)

    def piece_of(kind, line_of, x, back):
        if kind == 0:
            start = (x * nz + z_of(back)) * rows_two + (line_of * 2 + core) * piece
            return two.at[:, pl.ds(pl.multiple_of(start, piece), piece), :]
        start = z_of(back) * rows_three + ((line_of * 2 + core) * ny + x) * piece
        return three.at[kind - 1, :, pl.ds(pl.multiple_of(start, piece), piece), :]

    other_line, other_x = 1 - line, 1 - gy
    to_line = (other_line * 2 + core, gy, gz)
    to_x = (gx, other_x, gz)
    to_core = (line * 2 + 1 - core, gy, gz)
    BY_XY, BY_CORE, BY_Z, BY_STEM, BY_BACK = range(5)

    def remote(ref, route, arrival, device):
        return pltpu.make_async_remote_copy(
            src_ref=ref, dst_ref=ref, send_sem=sent.at[route], recv_sem=arrival,
            device_id=device, device_id_type=MESH,
        )

    def await_all(ref, route, arrival):
        remote(ref, route, arrival, to_core).wait_recv()

    total = {BY_XY: 0, BY_CORE: 0}

    def send(kind, line_of, x, back, route, arrival, device):
        total[route] += piece if kind == 0 else piece // TILES
        remote(piece_of(kind, line_of, x, back), route, arrival, device).start()

    def rows_of(kind, count):
        if kind == 0:
            return two.at[:, pl.ds(0, count * piece), :]
        return three.at[kind - 1, :, pl.ds(0, count * piece), :]

    def z_copy(kind, back, position):
        return remote(
            piece_of(kind, line, gy, back), BY_Z, z_recv.at[kind, z_of(back)],
            (gx, gy, mirrored(position)),
        )

    def z_start(kind):
        z_copy(kind, 0, 1 - depth).start()

        @pl.when(depth == 1)
        def _():
            z_copy(kind, 0, 2).start()

    def z_pass(kind, back):
        z_copy(kind, back, 0).wait_recv()

        @pl.when(depth == 1)
        def _():
            z_copy(kind, back, 2 if back < 2 else 0).start()

    def arrival_of(kind, name):
        if kind == 0:
            return two_recv.at[name]
        return three_recv.at[kind - 1, name]

    VIA_LINE, VIA_X, VIA_BOTH, VIA_CORE, STEP_X = range(5)

    def to_other_core(kind, line_of, x, back):
        send(kind, line_of, x, back, BY_CORE, arrival_of(kind, VIA_CORE), to_core)

    def two_from_z(step):
        if step > 0:
            z_pass(0, step)
        send(0, line, gy, step, BY_XY, arrival_of(0, STEP_X + step), to_x)
        if step > 0:
            send(0, line, gy, step, BY_XY, arrival_of(0, VIA_LINE), to_line)
            to_other_core(0, line, gy, step)

    def two_from_x(step):
        remote(rows_of(0, 1), BY_XY, arrival_of(0, STEP_X + step), to_x).wait_recv()
        send(0, line, other_x, step, BY_XY, arrival_of(0, VIA_BOTH), to_line)
        to_other_core(0, line, other_x, step)

    def two_from_line():
        await_all(rows_of(0, nz - 1), BY_XY, arrival_of(0, VIA_LINE))
        for step in range(1, nz):
            to_other_core(0, other_line, gy, step)

    def two_from_both():
        await_all(rows_of(0, nz), BY_XY, arrival_of(0, VIA_BOTH))
        for step in range(nz):
            to_other_core(0, other_line, other_x, step)

    def three_from_z(kind):
        for step in range(1, nz):
            z_pass(kind, step)
            send(kind, line, gy, step, BY_XY, arrival_of(kind, VIA_LINE), to_line)
            send(kind, line, gy, step, BY_XY, arrival_of(kind, VIA_X), to_x)
            to_other_core(kind, line, gy, step)

    def three_from_line(kind):
        await_all(rows_of(kind, nz - 1), BY_XY, arrival_of(kind, VIA_LINE))
        for step in range(1, nz):
            send(kind, other_line, gy, step, BY_XY, arrival_of(kind, VIA_BOTH), to_x)
            to_other_core(kind, other_line, gy, step)

    def three_from_x(kind):
        await_all(rows_of(kind, nz - 1), BY_XY, arrival_of(kind, VIA_X))
        for step in range(1, nz):
            to_other_core(kind, line, other_x, step)
        await_all(rows_of(kind, nz - 1), BY_XY, arrival_of(kind, VIA_BOTH))
        for step in range(1, nz):
            to_other_core(kind, other_line, other_x, step)

    def landing(index):
        return first.at[index // nz, :, index % nz]

    def stem_copy(step):
        target = (me + step) % devices
        return pltpu.make_async_remote_copy(
            src_ref=sorted_stem.at[target], dst_ref=landing(me),
            send_sem=sent.at[BY_STEM], recv_sem=bulk_recv.at[0],
            device_id=coordinates(target), device_id_type=MESH,
        )

    def send_stem(step, carry):
        stem_copy(step).start()
        return carry

    def sort_one(tile, carry):
        for part in range(2):
            moved = jnp.dot(
                one[slices[0], part], perm[tile], preferred_element_type=jnp.float32
            ).astype(jnp.bfloat16)
            for half in range(2):
                one_perm[2 * tile + half, :, part * LANE : (part + 1) * LANE] = moved[
                    :, half * LANE : (half + 1) * LANE
                ]
        return carry

    chunk = ROWS // group

    def contract_first(k, carry):
        operand = jnp.concatenate(
            [first[i].reshape(2 * ROWS, LANE) for i in range(group)], axis=1
        )
        for part, value in enumerate(complex_tile(operand, one_perm[k])):
            for c in range(nz):
                for ry in range(ny):
                    row, column = (c * ny + ry) * chunk, (ry * nz + c) * LANE
                    second[part, k, :, column : column + LANE] = value[row : row + chunk]
        return carry

    def contract_second(s, carry):
        operand = second[...].reshape(2 * ROWS, WIDTH)
        columns = pl.ds(pl.multiple_of(s * LANE, LANE), LANE)
        branch = jnp.concatenate([two[0, :, columns], two[1, :, columns]], axis=1)
        for part, value in enumerate(complex_tile(operand, branch)):
            for k in range(group):
                third[part, s, :, k * LANE : (k + 1) * LANE] = value[k * chunk : (k + 1) * chunk]
        return carry

    def back_copy(tile, step):
        target = (place + step) % group
        columns = pl.ds(tile * TILE, TILE)
        return pltpu.make_async_remote_copy(
            src_ref=result.at[target, :, :, columns], dst_ref=out.at[place, :, :, columns],
            send_sem=sent.at[BY_BACK], recv_sem=bulk_recv.at[1],
            device_id=(gx, target // nz, target % nz), device_id_type=MESH,
        )

    def contract_third(tile):
        await_all(rows_of(tile + 1, 4 * (nz - 1)), BY_CORE, arrival_of(tile + 1, VIA_CORE))
        operand = third[...].reshape(2 * ROWS, WIDTH)
        branch = jnp.concatenate([three[tile, 0], three[tile, 1]], axis=1)
        for part, value in enumerate(complex_tile(operand, branch)):
            result[:, part, :, tile * TILE : (tile + 1) * TILE] = value.reshape(group, chunk, TILE)

        def send_back(step, inner):
            back_copy(tile, step).start()
            return inner

        lax.fori_loop(1, group, send_back, 0)

    z_start(0)
    two_from_z(0)
    lax.fori_loop(1, devices, send_stem, 0)
    own = pltpu.make_async_copy(sorted_stem.at[me], landing(me), local_sem.at[1])
    own.start()
    for kind in range(1, TILES + 1):
        z_start(kind)
    load_one.wait()
    for step in range(1, nz):
        sort_one(step - 1, 0)
        two_from_z(step)
    sort_one(TILES - 1, 0)
    for step in range(nz):
        two_from_x(step)
    three_from_z(1)
    two_from_line()
    three_from_z(2)
    three_from_line(1)
    two_from_both()
    own.wait()
    blocks = sorted_stem.at[pl.ds(0, devices - 1)]
    await_all(blocks, BY_STEM, bulk_recv.at[0])
    lax.fori_loop(0, group, contract_first, 0)
    three_from_x(1)
    three_from_line(2)
    three_from_z(3)
    await_all(rows_of(0, 4 * nz - 2), BY_CORE, arrival_of(0, VIA_CORE))
    lax.fori_loop(0, group, contract_second, 0)
    three_from_z(4)
    three_from_line(3)
    three_from_x(2)
    contract_third(0)
    three_from_line(4)
    three_from_x(3)
    contract_third(1)
    three_from_x(4)
    contract_third(2)
    contract_third(3)
    keep = pltpu.make_async_copy(result.at[place], out.at[place], local_sem.at[1])
    keep.start()
    keep.wait()

    for route in (BY_XY, BY_CORE):
        remote(two.at[:, pl.ds(0, total[route]), :], route, bulk_recv.at[0], to_core).wait_send()

    @pl.when(depth == 0)
    def _():
        remote(rows_of(0, 2), BY_Z, bulk_recv.at[0], to_core).wait_send()

    @pl.when(depth == 1)
    def _():
        remote(rows_of(0, 10), BY_Z, bulk_recv.at[0], to_core).wait_send()

    remote(blocks, BY_STEM, bulk_recv.at[0], to_core).wait_send()
    returned = result.at[pl.ds(0, group - 1)]
    remote(returned, BY_BACK, bulk_recv.at[1], to_core).wait()


def fused_body(dims, stem, branch_one, branch_two, branch_three, slice_values):
    nx, ny, nz = dims
    group = ny * nz
    devices = nx * group
    chunk = ROWS // group
    bf16 = jnp.bfloat16
    vmem = pl.BlockSpec(memory_space=pltpu.VMEM)
    dma = pltpu.SemaphoreType.DMA
    blocks = pl.pallas_call(
        functools.partial(kernel, dims),
        out_shape=jax.ShapeDtypeStruct((group, 2, chunk, WIDTH), bf16),
        in_specs=[
            pl.BlockSpec(memory_space=pltpu.SMEM),
            vmem,
            pl.BlockSpec(memory_space=pl.ANY),
            vmem,
            vmem,
        ],
        out_specs=pl.BlockSpec(memory_space=pl.ANY),
        scratch_shapes=[
            pltpu.VMEM((WIDTH // TILE, WIDTH, TILE), bf16),
            pltpu.VMEM(branch_one.shape, bf16),
            pltpu.VMEM((group, WIDTH, 2 * LANE), bf16),
            pltpu.VMEM((2, WIDTH, WIDTH), bf16),
            pltpu.VMEM((TILES, 2, WIDTH, TILE), bf16),
            pltpu.VMEM((devices, 2, ROWS // nx, LANE), bf16),
            pltpu.VMEM((nx * ny, 2, nz, ROWS // nx, LANE), bf16),
            pltpu.VMEM((2, group, chunk, WIDTH), bf16),
            pltpu.VMEM((2, group, chunk, WIDTH), bf16),
            pltpu.VMEM((group, 2, chunk, WIDTH), bf16),
            dma((2,)),
            dma((1 + TILES, nz)),
            dma((4 + nz,)),
            dma((TILES, 4)),
            dma((2,)),
            dma((5,)),
        ],
        compiler_params=pltpu.CompilerParams(
            collective_id=0, has_side_effects=True, vmem_limit_bytes=VMEM_LIMIT
        ),
        cost_estimate=pl.CostEstimate(
            flops=24 * ROWS * WIDTH * WIDTH, bytes_accessed=16 * WIDTH * WIDTH, transcendentals=0
        ),
    )(slice_values, stem.reshape(2, ROWS, WIDTH), branch_one, branch_two, branch_three)
    return blocks.transpose(1, 2, 0, 3).reshape(stem.shape)


def solution(mesh):
    dims = (mesh.shape["gx"], mesh.shape["gy"], mesh.shape["gz"])
    group_one, group_two = dims[0] * dims[1], dims[1] * dims[2]
    fused = group_one == group_two == WIDTH // LANE and dims == (4, 2, 4)
    return jax.shard_map(
        functools.partial(fused_body, dims) if fused else body,
        mesh=mesh,
        in_specs=(
            P(None, "gx", "gy", "gz", None, None),
            P(),
            P(None, None, ("gy", "gz"), None),
            P(None, None, "gz", None),
            P(),
        ),
        out_specs=P(None, "gx", "gy", "gz", None, None),
        check_vma=False,
    )
```

time: 91.9 us -> 102 us (1.11); the launches traced: 90.5 us -> 102 us
  Pallas kernels: 87.7 us -> 99.2 us
    pallas_call x1, Pallas kernels: 87.7 us -> 99.2 us  [fused_body(): pl.pallas_call(functools.partial(kernel, dims), out_shape=jax.ShapeDtypeS...]
where the time goes in v1:
time: 102 us
  Pallas kernels  99.2 us (97%)
  local copies, waits for them, and re-layouts  2.77 us (3%)
    pallas_call x1, Pallas kernels, fused_body(): pl.pallas_call(functools.partial(kernel, dims), out_shape=jax.ShapeDtypeS...  99.2 us
    transpose x1, local copies, waits for them, and re-layouts, fused_body(): return blocks.transpose(1, 2, 0, 3).reshape(stem.shape)  2.77 us

profile of v1, /device:TPU:0, one launch (start us, length us, event | category | flops | bytes accessed | tf_op | source)
XLA Modules:
  0.0 101.9 jit_solution(13744943387487087019)
XLA Ops:
  0.0 99.2 %shard_map.55 = bf16[8,2,32,1024]{3,2,1,0:T(8,128)(2,1)} custom-call(s32[3]{0:T(128)} %slices.1, bf16[2,256,1024]{2,1,0:T(8,128)(2,1)} %bitcast.8, bf16[2,2,1024,1024]{3,2,1,0:T(8,128)(2,1)} %one_hbm.1, bf16[2,2,128,1024]{3,2,1,0:T(8,128)(2,1)} %two_in.1, bf16[2,2,256,1024]{3,2,1,0:T(8,128)(2,1)} %three_in.1), custom_call_target="tpu_custom_call" | custom-call | flops 6442450944 | bytes 16777216 | tf_op jit(solution)/shard_map/pallas_call | solution.py:422
  99.2 2.8 %copy.9 = bf16[2,32,8,1024]{3,2,1,0:T(8,128)(2,1)} copy(bf16[2,32,8,1024]{3,1,0,2:T(8,128)(2,1)} %bitcast.7) | data formatting | bytes 2097152 | tf_op jit(solution)/shard_map/transpose | solution.py:458

commit v2 on v1

--- a/solution.py
+++ b/solution.py
@@ -105,11 +105,13 @@
 
 
 TILES = WIDTH // TILE
+GROUPS = 2
+TILES_IN = TILES // GROUPS
 
 
 def kernel(
     dims, slices, stem, one_hbm, two_in, three_in, out,
-    perm, one, one_perm, two, three, sorted_stem, first, second, third, result,
+    perm, one, one_perm, two, three, sorted_stem, staged, first, second, third, result,
     local_sem, z_recv, two_recv, three_recv, bulk_recv, sent,
 ):
     nx, ny, nz = dims
@@ -159,7 +161,8 @@
         moved = moved.astype(jnp.bfloat16).reshape(2, nx, rows_one, TILE)
         for x in range(nx):
             for half in range(2):
-                sorted_stem[x * group + 2 * tile + half] = moved[
+                target = 2 * tile + half
+                sorted_stem[x * ny + target // nz, target % nz] = moved[
                     :, x, :, half * LANE : (half + 1) * LANE
                 ]
         return carry
@@ -181,7 +184,8 @@
             start = (x * nz + z_of(back)) * rows_two + (line_of * 2 + core) * piece
             return two.at[:, pl.ds(pl.multiple_of(start, piece), piece), :]
         start = z_of(back) * rows_three + ((line_of * 2 + core) * ny + x) * piece
-        return three.at[kind - 1, :, pl.ds(pl.multiple_of(start, piece), piece), :]
+        tiles = pl.ds(0, TILES) if kind < 0 else pl.ds((kind - 1) * TILES_IN, TILES_IN)
+        return three.at[tiles, :, pl.ds(pl.multiple_of(start, piece), piece), :]
 
     other_line, other_x = 1 - line, 1 - gy
     to_line = (other_line * 2 + core, gy, gz)
@@ -201,17 +205,17 @@
     total = {BY_XY: 0, BY_CORE: 0}
 
     def send(kind, line_of, x, back, route, arrival, device):
-        total[route] += piece if kind == 0 else piece // TILES
+        total[route] += piece if kind == 0 else piece // GROUPS
         remote(piece_of(kind, line_of, x, back), route, arrival, device).start()
 
     def rows_of(kind, count):
         if kind == 0:
             return two.at[:, pl.ds(0, count * piece), :]
-        return three.at[kind - 1, :, pl.ds(0, count * piece), :]
+        return three.at[pl.ds((kind - 1) * TILES_IN, TILES_IN), :, pl.ds(0, count * piece), :]
 
     def z_copy(kind, back, position):
         return remote(
-            piece_of(kind, line, gy, back), BY_Z, z_recv.at[kind, z_of(back)],
+            piece_of(kind, line, gy, back), BY_Z, z_recv.at[1 if kind else 0, z_of(back)],
             (gx, gy, mirrored(position)),
         )
 
@@ -234,69 +238,95 @@
             return two_recv.at[name]
         return three_recv.at[kind - 1, name]
 
-    VIA_LINE, VIA_X, VIA_BOTH, VIA_CORE, STEP_X = range(5)
+    VIA_CORE, VIA_LINE, VIA_X, VIA_BOTH = range(4)
+    TWO_LINE, TWO_X = VIA_X, VIA_X + nz + 1
 
     def to_other_core(kind, line_of, x, back):
         send(kind, line_of, x, back, BY_CORE, arrival_of(kind, VIA_CORE), to_core)
 
-    def two_from_z(step):
-        if step > 0:
-            z_pass(0, step)
-        send(0, line, gy, step, BY_XY, arrival_of(0, STEP_X + step), to_x)
-        if step > 0:
-            send(0, line, gy, step, BY_XY, arrival_of(0, VIA_LINE), to_line)
-            to_other_core(0, line, gy, step)
-
-    def two_from_x(step):
-        remote(rows_of(0, 1), BY_XY, arrival_of(0, STEP_X + step), to_x).wait_recv()
-        send(0, line, other_x, step, BY_XY, arrival_of(0, VIA_BOTH), to_line)
-        to_other_core(0, line, other_x, step)
-
-    def two_from_line():
-        await_all(rows_of(0, nz - 1), BY_XY, arrival_of(0, VIA_LINE))
-        for step in range(1, nz):
-            to_other_core(0, other_line, gy, step)
-
-    def two_from_both():
-        await_all(rows_of(0, nz), BY_XY, arrival_of(0, VIA_BOTH))
-        for step in range(nz):
-            to_other_core(0, other_line, other_x, step)
-
-    def three_from_z(kind):
+    def z_through(kind):
         for step in range(1, nz):
             z_pass(kind, step)
+
+    def two_spread(step):
+        send(0, line, gy, step, BY_XY, arrival_of(0, TWO_X + step), to_x)
+        if step > 0:
+            send(0, line, gy, step, BY_XY, arrival_of(0, TWO_LINE + step), to_line)
+            to_other_core(0, line, gy, step)
+
+    def two_from_x(step):
+        await_all(rows_of(0, 1), BY_XY, arrival_of(0, TWO_X + step))
+        if step < nz // 2:
+            send(0, line, other_x, step, BY_XY, arrival_of(0, VIA_LINE), to_line)
+        to_other_core(0, line, other_x, step)
+
+    def two_from_line(step):
+        await_all(rows_of(0, 1), BY_XY, arrival_of(0, TWO_LINE + step))
+        if step >= nz // 2:
+            send(0, other_line, gy, step, BY_XY, arrival_of(0, TWO_LINE), to_x)
+        to_other_core(0, other_line, gy, step)
+
+    def two_from_both():
+        await_all(rows_of(0, nz // 2), BY_XY, arrival_of(0, VIA_LINE))
+        for step in range(nz // 2):
+            to_other_core(0, other_line, other_x, step)
+        await_all(rows_of(0, nz // 2), BY_XY, arrival_of(0, TWO_LINE))
+        for step in range(nz // 2, nz):
+            to_other_core(0, other_line, other_x, step)
+
+    def three_spread(kind):
+        for step in range(1, nz):
             send(kind, line, gy, step, BY_XY, arrival_of(kind, VIA_LINE), to_line)
             send(kind, line, gy, step, BY_XY, arrival_of(kind, VIA_X), to_x)
+        for step in range(1, nz):
             to_other_core(kind, line, gy, step)
 
-    def three_from_line(kind):
-        await_all(rows_of(kind, nz - 1), BY_XY, arrival_of(kind, VIA_LINE))
+    def three_turn(kind):
+        if kind % 2 == 1:
+            await_all(rows_of(kind, nz - 1), BY_XY, arrival_of(kind, VIA_LINE))
+            near, far = (other_line, gy), to_x
+        else:
+            await_all(rows_of(kind, nz - 1), BY_XY, arrival_of(kind, VIA_X))
+            near, far = (line, other_x), to_line
         for step in range(1, nz):
-            send(kind, other_line, gy, step, BY_XY, arrival_of(kind, VIA_BOTH), to_x)
-            to_other_core(kind, other_line, gy, step)
-
-    def three_from_x(kind):
-        await_all(rows_of(kind, nz - 1), BY_XY, arrival_of(kind, VIA_X))
+            send(kind, *near, step, BY_XY, arrival_of(kind, VIA_BOTH), far)
+            to_other_core(kind, *near, step)
+
+    def three_last(kind):
+        if kind % 2 == 1:
+            await_all(rows_of(kind, nz - 1), BY_XY, arrival_of(kind, VIA_X))
+            near = (line, other_x)
+        else:
+            await_all(rows_of(kind, nz - 1), BY_XY, arrival_of(kind, VIA_LINE))
+            near = (other_line, gy)
         for step in range(1, nz):
-            to_other_core(kind, line, other_x, step)
+            to_other_core(kind, *near, step)
         await_all(rows_of(kind, nz - 1), BY_XY, arrival_of(kind, VIA_BOTH))
         for step in range(1, nz):
             to_other_core(kind, other_line, other_x, step)
 
-    def landing(index):
-        return first.at[index // nz, :, index % nz]
-
-    def stem_copy(step):
-        target = (me + step) % devices
-        return pltpu.make_async_remote_copy(
-            src_ref=sorted_stem.at[target], dst_ref=landing(me),
+    spot = gx * ny + gy
+    plane = nx * ny
+
+    def stem_in_plane(step, carry):
+        target = (spot + step) % plane
+        pltpu.make_async_remote_copy(
+            src_ref=sorted_stem.at[target], dst_ref=staged.at[spot],
             send_sem=sent.at[BY_STEM], recv_sem=bulk_recv.at[0],
-            device_id=coordinates(target), device_id_type=MESH,
-        )
-
-    def send_stem(step, carry):
-        stem_copy(step).start()
-        return carry
+            device_id=(target // ny, target % ny, gz), device_id_type=MESH,
+        ).start()
+        return carry
+
+    def stem_over_z(hop):
+        z = (gz + hop) % nz
+        pltpu.make_async_remote_copy(
+            src_ref=staged.at[:, z], dst_ref=first.at[:, gz],
+            send_sem=sent.at[BY_STEM], recv_sem=bulk_recv.at[2],
+            device_id=(gx, gy, z), device_id_type=MESH,
+        ).start()
+
+    def block_bytes(count):
+        return two.at[:, pl.ds(0, count * 8), :]
 
     def sort_one(tile, carry):
         for part in range(2):
@@ -313,7 +343,7 @@
 
     def contract_first(k, carry):
         operand = jnp.concatenate(
-            [first[i].reshape(2 * ROWS, LANE) for i in range(group)], axis=1
+            [first[i].swapaxes(0, 1).reshape(2 * ROWS, LANE) for i in range(plane)], axis=1
         )
         for part, value in enumerate(complex_tile(operand, one_perm[k])):
             for c in range(nz):
@@ -322,13 +352,16 @@
                     second[part, k, :, column : column + LANE] = value[row : row + chunk]
         return carry
 
-    def contract_second(s, carry):
+    def contract_second(pair, carry):
         operand = second[...].reshape(2 * ROWS, WIDTH)
-        columns = pl.ds(pl.multiple_of(s * LANE, LANE), LANE)
+        columns = pl.ds(pl.multiple_of(pair * 2 * LANE, 2 * LANE), 2 * LANE)
         branch = jnp.concatenate([two[0, :, columns], two[1, :, columns]], axis=1)
         for part, value in enumerate(complex_tile(operand, branch)):
-            for k in range(group):
-                third[part, s, :, k * LANE : (k + 1) * LANE] = value[k * chunk : (k + 1) * chunk]
+            for half in range(2):
+                for k in range(group):
+                    third[part, 2 * pair + half, :, k * LANE : (k + 1) * LANE] = value[
+                        k * chunk : (k + 1) * chunk, half * LANE : (half + 1) * LANE
+                    ]
         return carry
 
     def back_copy(tile, step):
@@ -341,7 +374,9 @@
         )
 
     def contract_third(tile):
-        await_all(rows_of(tile + 1, 4 * (nz - 1)), BY_CORE, arrival_of(tile + 1, VIA_CORE))
+        if tile % TILES_IN == 0:
+            kind = tile // TILES_IN + 1
+            await_all(rows_of(kind, 4 * (nz - 1)), BY_CORE, arrival_of(kind, VIA_CORE))
         operand = third[...].reshape(2 * ROWS, WIDTH)
         branch = jnp.concatenate([three[tile, 0], three[tile, 1]], axis=1)
         for part, value in enumerate(complex_tile(operand, branch)):
@@ -354,41 +389,53 @@
         lax.fori_loop(1, group, send_back, 0)
 
     z_start(0)
-    two_from_z(0)
-    lax.fori_loop(1, devices, send_stem, 0)
-    own = pltpu.make_async_copy(sorted_stem.at[me], landing(me), local_sem.at[1])
+    two_spread(0)
+    z_start(-1)
+    own = pltpu.make_async_copy(sorted_stem.at[spot], staged.at[spot], local_sem.at[1])
     own.start()
-    for kind in range(1, TILES + 1):
-        z_start(kind)
     load_one.wait()
-    for step in range(1, nz):
-        sort_one(step - 1, 0)
-        two_from_z(step)
-    sort_one(TILES - 1, 0)
-    for step in range(nz):
-        two_from_x(step)
-    three_from_z(1)
-    two_from_line()
-    three_from_z(2)
-    three_from_line(1)
+    z_pass(0, 1)
+    lax.fori_loop(1, plane, stem_in_plane, 0)
+    two_spread(1)
+    z_pass(-1, 1)
+    two_from_x(0)
+    sort_one(0, 0)
+    z_pass(0, 2)
+    two_spread(2)
+    z_pass(0, 3)
+    two_spread(3)
+    z_pass(-1, 2)
+    two_from_x(1)
+    two_from_line(1)
+    z_pass(-1, 3)
+    own.wait()
+    await_all(block_bytes((plane - 1) * nz), BY_STEM, bulk_recv.at[0])
+    for hop in (2, 1, 3):
+        stem_over_z(hop)
+    own = pltpu.make_async_copy(staged.at[:, gz], first.at[:, gz], local_sem.at[1])
+    own.start()
+    three_spread(1)
+    two_from_x(2)
+    two_from_line(2)
+    two_from_x(3)
+    two_from_line(3)
+    sort_one(1, 0)
+    sort_one(2, 0)
+    sort_one(3, 0)
+    three_turn(1)
+    three_spread(2)
     two_from_both()
+    three_last(1)
     own.wait()
-    blocks = sorted_stem.at[pl.ds(0, devices - 1)]
-    await_all(blocks, BY_STEM, bulk_recv.at[0])
+    await_all(block_bytes((nz - 1) * plane), BY_STEM, bulk_recv.at[2])
     lax.fori_loop(0, group, contract_first, 0)
-    three_from_x(1)
-    three_from_line(2)
-    three_from_z(3)
+    three_turn(2)
     await_all(rows_of(0, 4 * nz - 2), BY_CORE, arrival_of(0, VIA_CORE))
-    lax.fori_loop(0, group, contract_second, 0)
-    three_from_z(4)
-    three_from_line(3)
-    three_from_x(2)
+    lax.fori_loop(0, 2, contract_second, 0)
+    lax.fori_loop(2, 4, contract_second, 0)
     contract_third(0)
-    three_from_line(4)
-    three_from_x(3)
     contract_third(1)
-    three_from_x(4)
+    three_last(2)
     contract_third(2)
     contract_third(3)
     keep = pltpu.make_async_copy(result.at[place], out.at[place], local_sem.at[1])
@@ -406,7 +453,7 @@
     def _():
         remote(rows_of(0, 10), BY_Z, bulk_recv.at[0], to_core).wait_send()
 
-    remote(blocks, BY_STEM, bulk_recv.at[0], to_core).wait_send()
+    remote(block_bytes((plane - 1) * nz + (nz - 1) * plane), BY_STEM, bulk_recv.at[0], to_core).wait_send()
     returned = result.at[pl.ds(0, group - 1)]
     remote(returned, BY_BACK, bulk_recv.at[1], to_core).wait()
 
@@ -436,16 +483,17 @@
             pltpu.VMEM((group, WIDTH, 2 * LANE), bf16),
             pltpu.VMEM((2, WIDTH, WIDTH), bf16),
             pltpu.VMEM((TILES, 2, WIDTH, TILE), bf16),
-            pltpu.VMEM((devices, 2, ROWS // nx, LANE), bf16),
-            pltpu.VMEM((nx * ny, 2, nz, ROWS // nx, LANE), bf16),
+            pltpu.VMEM((nx * ny, nz, 2, ROWS // nx, LANE), bf16),
+            pltpu.VMEM((nx * ny, nz, 2, ROWS // nx, LANE), bf16),
+            pltpu.VMEM((nx * ny, nz, 2, ROWS // nx, LANE), bf16),
             pltpu.VMEM((2, group, chunk, WIDTH), bf16),
             pltpu.VMEM((2, group, chunk, WIDTH), bf16),
             pltpu.VMEM((group, 2, chunk, WIDTH), bf16),
             dma((2,)),
-            dma((1 + TILES, nz)),
-            dma((4 + nz,)),
-            dma((TILES, 4)),
-            dma((2,)),
+            dma((2, nz)),
+            dma((3 + 2 * nz,)),
+            dma((GROUPS, 4)),
+            dma((3,)),
             dma((5,)),
         ],
         compiler_params=pltpu.CompilerParams(

time: 102 us -> 85.1 us (0.83)
  Pallas kernels: 99.2 us -> 82.1 us
    pallas_call x1, Pallas kernels: 99.2 us -> 82.1 us  [fused_body(): pl.pallas_call(functools.partial(kernel, dims), out_shape=jax.ShapeDtypeS...]
where the time goes in v2:
time: 85.1 us; the launch traced here: 84.9 us
  Pallas kernels  82.1 us (96%)
  local copies, waits for them, and re-layouts  2.77 us (3%)
    pallas_call x1, Pallas kernels, fused_body(): pl.pallas_call(functools.partial(kernel, dims), out_shape=jax.ShapeDtypeS...  82.1 us
    transpose x1, local copies, waits for them, and re-layouts, fused_body(): return blocks.transpose(1, 2, 0, 3).reshape(stem.shape)  2.77 us

profile of v2, /device:TPU:0, one launch (start us, length us, event | category | flops | bytes accessed | tf_op | source)
XLA Modules:
  0.0 84.9 jit_solution(6037770320015156262)
XLA Ops:
  0.0 82.1 %shard_map.55 = bf16[8,2,32,1024]{3,2,1,0:T(8,128)(2,1)} custom-call(s32[3]{0:T(128)} %slices.1, bf16[2,256,1024]{2,1,0:T(8,128)(2,1)} %bitcast.8, bf16[2,2,1024,1024]{3,2,1,0:T(8,128)(2,1)} %one_hbm.1, bf16[2,2,128,1024]{3,2,1,0:T(8,128)(2,1)} %two_in.1, bf16[2,2,256,1024]{3,2,1,0:T(8,128)(2,1)} %three_in.1), custom_call_target="tpu_custom_call" | custom-call | flops 6442450944 | bytes 16777216 | tf_op jit(solution)/shard_map/pallas_call | solution.py:469
  82.1 2.8 %copy.9 = bf16[2,32,8,1024]{3,2,1,0:T(8,128)(2,1)} copy(bf16[2,32,8,1024]{3,1,0,2:T(8,128)(2,1)} %bitcast.7) | data formatting | bytes 2097152 | tf_op jit(solution)/shard_map/transpose | solution.py:506

commit v3 on v2

--- a/solution.py
+++ b/solution.py
@@ -116,27 +116,39 @@
 ):
     nx, ny, nz = dims
     group = ny * nz
-    devices = nx * group
     gx, gy, gz = lax.axis_index("gx"), lax.axis_index("gy"), lax.axis_index("gz")
     line, core = gx // 2, gx % 2
-    me = (gx * ny + gy) * nz + gz
     place = gy * nz + gz
 
     load_one = pltpu.make_async_copy(one_hbm, one, local_sem.at[0])
     load_one.start()
 
-    def coordinates(index):
-        return (index // group, (index // nz) % ny, index % nz)
-
     barrier = pltpu.get_barrier_semaphore()
 
-    def greet(step, carry):
-        pl.semaphore_signal(
-            barrier, inc=1, device_id=coordinates((me + step) % devices), device_id_type=MESH
-        )
-        return carry
-
-    lax.fori_loop(1, devices, greet, 0)
+    upper = gz // 2
+    depth = gz + upper * (nz - 1 - 2 * gz)
+
+    def mirrored(position):
+        return position + upper * (nz - 1 - 2 * position)
+
+    spot = gx * ny + gy
+    plane = nx * ny
+
+    def greet(device):
+        pl.semaphore_signal(barrier, inc=1, device_id=device, device_id_type=MESH)
+
+    def greet_plane(step, carry):
+        target = (spot + step) % plane
+        greet((target // ny, target % ny, gz))
+        return carry
+
+    greet((gx, gy, mirrored(1 - depth)))
+
+    @pl.when(depth == 1)
+    def _():
+        greet((gx, gy, mirrored(2)))
+
+    lax.fori_loop(1, plane, greet_plane, 0)
 
     rows_two, rows_three = WIDTH // group, WIDTH // nz
     piece = rows_two // nx
@@ -167,14 +179,7 @@
                 ]
         return carry
 
-    lax.fori_loop(0, TILES, sort_stem, 0)
-    pl.semaphore_wait(barrier, devices - 1)
-
-    upper = gz // 2
-    depth = gz + upper * (nz - 1 - 2 * gz)
-
-    def mirrored(position):
-        return position + upper * (nz - 1 - 2 * position)
+    pl.semaphore_wait(barrier, plane + depth)
 
     def z_of(back):
         return gz if back == 0 else mirrored(1 - depth if back == 1 else back)
@@ -305,9 +310,6 @@
         for step in range(1, nz):
             to_other_core(kind, other_line, other_x, step)
 
-    spot = gx * ny + gy
-    plane = nx * ny
-
     def stem_in_plane(step, carry):
         target = (spot + step) % plane
         pltpu.make_async_remote_copy(
@@ -317,8 +319,8 @@
         ).start()
         return carry
 
-    def stem_over_z(hop):
-        z = (gz + hop) % nz
+    def stem_over_z(position):
+        z = mirrored(position)
         pltpu.make_async_remote_copy(
             src_ref=staged.at[:, z], dst_ref=first.at[:, gz],
             send_sem=sent.at[BY_STEM], recv_sem=bulk_recv.at[2],
@@ -391,27 +393,29 @@
     z_start(0)
     two_spread(0)
     z_start(-1)
+    lax.fori_loop(0, TILES, sort_stem, 0)
+    lax.fori_loop(1, plane, stem_in_plane, 0)
     own = pltpu.make_async_copy(sorted_stem.at[spot], staged.at[spot], local_sem.at[1])
     own.start()
-    load_one.wait()
     z_pass(0, 1)
-    lax.fori_loop(1, plane, stem_in_plane, 0)
     two_spread(1)
     z_pass(-1, 1)
     two_from_x(0)
+    load_one.wait()
     sort_one(0, 0)
     z_pass(0, 2)
     two_spread(2)
     z_pass(0, 3)
     two_spread(3)
     z_pass(-1, 2)
+    own.wait()
+    await_all(block_bytes((plane - 1) * nz), BY_STEM, bulk_recv.at[0])
+    stem_over_z(2)
     two_from_x(1)
     two_from_line(1)
     z_pass(-1, 3)
-    own.wait()
-    await_all(block_bytes((plane - 1) * nz), BY_STEM, bulk_recv.at[0])
-    for hop in (2, 1, 3):
-        stem_over_z(hop)
+    stem_over_z(3)
+    stem_over_z(1 - depth)
     own = pltpu.make_async_copy(staged.at[:, gz], first.at[:, gz], local_sem.at[1])
     own.start()
     three_spread(1)

time: 85.1 us -> 81.1 us (0.953)
  Pallas kernels: 82.1 us -> 78.1 us
    pallas_call x1, Pallas kernels: 82.1 us -> 78.1 us  [fused_body(): pl.pallas_call(functools.partial(kernel, dims), out_shape=jax.ShapeDtypeS...]
where the time goes in v3:
time: 81.1 us; the launch traced here: 80.9 us
  Pallas kernels  78.1 us (96%)
  local copies, waits for them, and re-layouts  2.77 us (3%)
    pallas_call x1, Pallas kernels, fused_body(): pl.pallas_call(functools.partial(kernel, dims), out_shape=jax.ShapeDtypeS...  78.1 us
    transpose x1, local copies, waits for them, and re-layouts, fused_body(): return blocks.transpose(1, 2, 0, 3).reshape(stem.shape)  2.77 us

profile of v3, /device:TPU:0, one launch (start us, length us, event | category | flops | bytes accessed | tf_op | source)
XLA Modules:
  0.0 80.9 jit_solution(1708767838107193871)
XLA Ops:
  0.0 78.1 %shard_map.55 = bf16[8,2,32,1024]{3,2,1,0:T(8,128)(2,1)} custom-call(s32[3]{0:T(128)} %slices.1, bf16[2,256,1024]{2,1,0:T(8,128)(2,1)} %bitcast.8, bf16[2,2,1024,1024]{3,2,1,0:T(8,128)(2,1)} %one_hbm.1, bf16[2,2,128,1024]{3,2,1,0:T(8,128)(2,1)} %two_in.1, bf16[2,2,256,1024]{3,2,1,0:T(8,128)(2,1)} %three_in.1), custom_call_target="tpu_custom_call" | custom-call | flops 6442450944 | bytes 16777216 | tf_op jit(solution)/shard_map/pallas_call | solution.py:473
  78.1 2.8 %copy.9 = bf16[2,32,8,1024]{3,2,1,0:T(8,128)(2,1)} copy(bf16[2,32,8,1024]{3,1,0,2:T(8,128)(2,1)} %bitcast.7) | data formatting | bytes 2097152 | tf_op jit(solution)/shard_map/transpose | solution.py:510

commit v4 on v3

--- a/solution.py
+++ b/solution.py
@@ -405,17 +405,17 @@
     sort_one(0, 0)
     z_pass(0, 2)
     two_spread(2)
+    own.wait()
+    await_all(block_bytes((plane - 1) * nz), BY_STEM, bulk_recv.at[0])
+    stem_over_z(2)
     z_pass(0, 3)
     two_spread(3)
     z_pass(-1, 2)
-    own.wait()
-    await_all(block_bytes((plane - 1) * nz), BY_STEM, bulk_recv.at[0])
-    stem_over_z(2)
     two_from_x(1)
     two_from_line(1)
     z_pass(-1, 3)
+    stem_over_z(1 - depth)
     stem_over_z(3)
-    stem_over_z(1 - depth)
     own = pltpu.make_async_copy(staged.at[:, gz], first.at[:, gz], local_sem.at[1])
     own.start()
     three_spread(1)
@@ -429,13 +429,13 @@
     three_turn(1)
     three_spread(2)
     two_from_both()
-    three_last(1)
     own.wait()
     await_all(block_bytes((nz - 1) * plane), BY_STEM, bulk_recv.at[2])
     lax.fori_loop(0, group, contract_first, 0)
-    three_turn(2)
+    three_last(1)
     await_all(rows_of(0, 4 * nz - 2), BY_CORE, arrival_of(0, VIA_CORE))
     lax.fori_loop(0, 2, contract_second, 0)
+    three_turn(2)
     lax.fori_loop(2, 4, contract_second, 0)
     contract_third(0)
     contract_third(1)

time: 81.1 us -> 79.3 us (0.978)
  Pallas kernels: 78.1 us -> 76.4 us
    pallas_call x1, Pallas kernels: 78.1 us -> 76.4 us  [fused_body(): pl.pallas_call(functools.partial(kernel, dims), out_shape=jax.ShapeDtypeS...]
where the time goes in v4:
time: 79.3 us; the launch traced here: 79.2 us
  Pallas kernels  76.4 us (96%)
  local copies, waits for them, and re-layouts  2.77 us (3%)
    pallas_call x1, Pallas kernels, fused_body(): pl.pallas_call(functools.partial(kernel, dims), out_shape=jax.ShapeDtypeS...  76.4 us
    transpose x1, local copies, waits for them, and re-layouts, fused_body(): return blocks.transpose(1, 2, 0, 3).reshape(stem.shape)  2.77 us

profile of v4, /device:TPU:0, one launch (start us, length us, event | category | flops | bytes accessed | tf_op | source)
XLA Modules:
  0.0 79.2 jit_solution(2370200397442493047)
XLA Ops:
  0.0 76.4 %shard_map.55 = bf16[8,2,32,1024]{3,2,1,0:T(8,128)(2,1)} custom-call(s32[3]{0:T(128)} %slices.1, bf16[2,256,1024]{2,1,0:T(8,128)(2,1)} %bitcast.8, bf16[2,2,1024,1024]{3,2,1,0:T(8,128)(2,1)} %one_hbm.1, bf16[2,2,128,1024]{3,2,1,0:T(8,128)(2,1)} %two_in.1, bf16[2,2,256,1024]{3,2,1,0:T(8,128)(2,1)} %three_in.1), custom_call_target="tpu_custom_call" | custom-call | flops 6442450944 | bytes 16777216 | tf_op jit(solution)/shard_map/pallas_call | solution.py:473
  76.4 2.8 %copy.9 = bf16[2,32,8,1024]{3,2,1,0:T(8,128)(2,1)} copy(bf16[2,32,8,1024]{3,1,0,2:T(8,128)(2,1)} %bitcast.7) | data formatting | bytes 2097152 | tf_op jit(solution)/shard_map/transpose | solution.py:510

commit v5 on v4

--- a/solution.py
+++ b/solution.py
@@ -435,8 +435,8 @@
     three_last(1)
     await_all(rows_of(0, 4 * nz - 2), BY_CORE, arrival_of(0, VIA_CORE))
     lax.fori_loop(0, 2, contract_second, 0)
+    lax.fori_loop(2, 4, contract_second, 0)
     three_turn(2)
-    lax.fori_loop(2, 4, contract_second, 0)
     contract_third(0)
     contract_third(1)
     three_last(2)

time: 79.3 us -> 79.1 us (level)
  no operation moved by 1% of the time
where the time goes in v5:
time: 79.1 us; the launch traced here: 78.9 us
  Pallas kernels  76.1 us (96%)
  local copies, waits for them, and re-layouts  2.77 us (4%)
    pallas_call x1, Pallas kernels, fused_body(): pl.pallas_call(functools.partial(kernel, dims), out_shape=jax.ShapeDtypeS...  76.1 us
    transpose x1, local copies, waits for them, and re-layouts, fused_body(): return blocks.transpose(1, 2, 0, 3).reshape(stem.shape)  2.77 us

profile of v5, /device:TPU:0, one launch (start us, length us, event | category | flops | bytes accessed | tf_op | source)
XLA Modules:
  0.0 78.9 jit_solution(6340561437290694215)
XLA Ops:
  0.0 76.1 %shard_map.55 = bf16[8,2,32,1024]{3,2,1,0:T(8,128)(2,1)} custom-call(s32[3]{0:T(128)} %slices.1, bf16[2,256,1024]{2,1,0:T(8,128)(2,1)} %bitcast.8, bf16[2,2,1024,1024]{3,2,1,0:T(8,128)(2,1)} %one_hbm.1, bf16[2,2,128,1024]{3,2,1,0:T(8,128)(2,1)} %two_in.1, bf16[2,2,256,1024]{3,2,1,0:T(8,128)(2,1)} %three_in.1), custom_call_target="tpu_custom_call" | custom-call | flops 6442450944 | bytes 16777216 | tf_op jit(solution)/shard_map/pallas_call | solution.py:473
  76.2 2.8 %copy.9 = bf16[2,32,8,1024]{3,2,1,0:T(8,128)(2,1)} copy(bf16[2,32,8,1024]{3,1,0,2:T(8,128)(2,1)} %bitcast.7) | data formatting | bytes 2097152 | tf_op jit(solution)/shard_map/transpose | solution.py:510
